TPU v7x, 32 devices: a whole 2x2x4 slice. The times are simulated.
32 devices in a mesh: row: 4 (over y, x), col: 8 (over z, core).
Axes of the slice: x: 2, y: 2, z: 4, core: 2. Of those that a mesh axis runs over, the one named last changes fastest.
Arguments:
- panel: bfloat16 [4, 4, 512, 512], P(None, 'row', 'col'), may hold values from -1.1953125 to 1.1953125
- inverse_factor: bfloat16 [512, 512], replicated
- slot_rows: int32 [4, 8, 2], P('row', 'col'), may hold values from 0 to 15, as said below
- slot_cols: int32 [4, 8, 2], P('row', 'col'), may hold values from 0 to 15, as said below
- live_count: int32 [4, 8], P('row', 'col'), may hold values from 0 to 2
Outputs:
- contrib: bfloat16 [4, 8, 2, 512, 512], P('row', 'col')
Inputs may be any that keep to these rules, and one draw needn't show every extreme that they name: slot_rows[r, c, s] is congruent to r modulo 4; for s < live_count[r, c] the slots of one position name distinct blocks with slot_rows >= slot_cols; the other slots are ignored. slot_cols[r, c, s] is congruent to c modulo 8.
All inputs are finite; a program needn't handle non-finite values.
Results may differ from a plain program's by a relative error of at most 0.0054.
Values may be sent and summed in bfloat16 or wider, within the bound.
A program may use at most 64 MiB of HBM per device.

v0:
```python
import jax
import jax.numpy as jnp
from jax import lax
from jax.sharding import PartitionSpec as P


def broadcast(value, axis, source):
    kept = jnp.where(lax.axis_index(axis) == source, value, 0).astype(value.dtype)
    return lax.psum(kept, axis)


def body(panel, inverse_factor, slot_rows, slot_cols, live_count):
    panel_count, _, part_rows, tile_width = panel.shape
    grid_rows = lax.axis_size("row")
    grid_cols = lax.axis_size("col")
    col_ratio = grid_cols // grid_rows
    column_count = panel_count // col_ratio
    solved = jnp.dot(
        panel.reshape(-1, tile_width), inverse_factor, preferred_element_type=jnp.float32
    )
    solved = solved.astype(jnp.bfloat16).reshape(panel_count, 1, part_rows, tile_width)
    row_blocks = lax.all_gather(solved, "col", axis=2, tiled=True).reshape(
        panel_count, tile_width, tile_width
    )
    position = lax.axis_index("col")
    grouped = row_blocks.reshape(column_count, col_ratio, tile_width, tile_width)
    picked = lax.dynamic_index_in_dim(grouped, position // grid_rows, 1, keepdims=False)
    col_blocks = broadcast(picked, "row", position % grid_rows)
    slot_total = slot_rows.shape[-1]
    rows_here = slot_rows.reshape(-1)
    cols_here = slot_cols.reshape(-1)
    live_here = live_count.reshape(())
    result = jnp.zeros((slot_total, tile_width, tile_width), jnp.bfloat16)

    def update(slot, current):
        left_tile = lax.dynamic_index_in_dim(
            row_blocks, rows_here[slot] // grid_rows, 0, keepdims=False
        )
        right_tile = lax.dynamic_index_in_dim(
            col_blocks, cols_here[slot] // grid_cols, 0, keepdims=False
        )
        product = lax.dot_general(
            left_tile, right_tile, (((1,), (1,)), ((), ())), preferred_element_type=jnp.float32
        )
        return lax.dynamic_update_index_in_dim(current, (-product).astype(jnp.bfloat16), slot, 0)

    result = lax.fori_loop(0, live_here, update, result)
    return result.reshape(1, 1, slot_total, tile_width, tile_width)


def solution(mesh):
    placed = (
        P(None, "row", "col", None),
        P(),
        P("row", "col", None),
        P("row", "col", None),
        P("row", "col"),
    )
    return jax.shard_map(
        body,
        mesh=mesh,
        in_specs=placed,
        out_specs=P("row", "col", None, None, None),
        check_vma=False,
    )
```

profile of v0, /device:TPU:17, one launch (start us, length us, event | category | flops | bytes accessed | tf_op | source)
XLA Modules:
  0.0 121.1 jit_solution(10737484094520950610)
XLA Ops:
  6.5 0.0 copy-start
  6.5 0.0 all-gather.2.cloned.1.call-start
  6.5 1.0 copy-done
  7.6 2.0 %convolution_convert_fusion = bf16[256,512]{1,0:T(8,128)(2,1)} fusion(bf16[256,512]{1,0:T(8,128)(2,1)} %bitcast.37, bf16[512,512]{1,0:T(8,128)(2,1)S(1)} %copy-done), kind=kOutput, calls=%fused_computation.9 | convolution fusion | flops 134348800 | bytes 1048576 | tf_op jit(solution)/shard_map/dot_general | solution.py:18
  9.5 0.0 all-gather.2.cloned.1.call-update
  9.6 0.0 all-reduce.2.cloned.1.call-start
  9.6 30.2 %all-gather.2.cloned.1.call-done = bf16[4,1,512,512]{3,2,0,1:T(8,128)(2,1)} async-done(((bf16[4,1,64,512]{3,2,0,1:T(8,128)(2,1)}), bf16[4,1,512,512]{3,2,0,1:T(8,128)(2,1)}) %all-gather.2.cloned.1.call-update) | async-done | bytes 2097168 | tf_op jit(solution)/shard_map/all_gather | solution.py:22
  39.8 0.0 copy-start.2
  39.8 0.0 copy-start.3
  39.8 2.3 %select_bitcast_fusion = bf16[2,512,512]{2,1,0:T(8,128)(2,1)} fusion(bf16[2,2,512,512]{3,2,1,0:T(8,128)(2,1)} %bitcast.35, s32[]{:T(128)S(6)} %select_n.71, pred[]{:T(512)S(6)} %eq.5), kind=kLoop, calls=%fused_computation.10 | loop fusion | flops 524288 | bytes 2097157 | tf_op jit(solution)/shard_map/jit(_where)/select_n | solution.py:8
  42.1 0.0 all-reduce.2.cloned.1.call-update
  42.1 52.9 %all-reduce.2.cloned.1.call-done = bf16[2,512,512]{2,1,0:T(8,128)(2,1)} async-done(((bf16[2,512,512]{2,1,0:T(8,128)(2,1)}), bf16[2,512,512]{2,1,0:T(8,128)(2,1)}) %all-reduce.2.cloned.1.call-update) | async-done | bytes 1048592 | tf_op jit(solution)/shard_map/psum | solution.py:9
  95.0 0.1 broadcast_in_dim.15
  95.1 0.0 copy-done.2
  95.1 0.0 copy-done.3
  95.1 18.1 %while.13 = (s32[]{:T(128)}, bf16[2,512,512]{2,1,0:T(8,128)(2,1)S(1)}, s32[]{:T(128)}, s32[2]{0:T(128)S(1)}, bf16[4,512,512]{2,1,0:T(8,128)(2,1)}, /*index=5*/s3...) while((s32[]{:T(128)}, ...), condition=%wide.region_2.3_spmd, body=%wide.region_1.2_spmd.sunk | while | flops 268959776 | bytes 1573443 | solution.py:47
  95.8 0.6 dynamic_slice.51
  99.0 0.6 dynamic_slice.50
  102.2 1.7 %fusion.15 = bf16[2,512,512]{2,1,0:T(8,128)(2,1)S(1)} fusion(bf16[2,512,512]{2,1,0:T(8,128)(2,1)S(1)} %get-tuple-element.198, s32[]{:T(128)S(6)} %select_n.81, bf16[2,512,512]{2,1,0:T(8,128)(2,1)} %get-tuple-element.217, s32[]{:T(128)S(6)} %select_n.83, bf16[4,512,512]{2,1,0:T(8,128)(2,1)} %get-tuple-element.215, s32[]{:T(128)S(6)} %select_n.85), kind=kOutput, calls=%fused_computation.3.clone.1 | convolution fusion | flops 268959744 | bytes 1572876 | tf_op jit(solution)/shard_map/while/body/dot_general | solution.py:42
  104.5 0.6 dynamic_slice.51
  107.7 0.6 dynamic_slice.50
  110.9 1.7 %fusion.15 = bf16[2,512,512]{2,1,0:T(8,128)(2,1)S(1)} fusion(bf16[2,512,512]{2,1,0:T(8,128)(2,1)S(1)} %get-tuple-element.198, s32[]{:T(128)S(6)} %select_n.81, bf16[2,512,512]{2,1,0:T(8,128)(2,1)} %get-tuple-element.217, s32[]{:T(128)S(6)} %select_n.83, bf16[4,512,512]{2,1,0:T(8,128)(2,1)} %get-tuple-element.215, s32[]{:T(128)S(6)} %select_n.85), kind=kOutput, calls=%fused_computation.3.clone.1 | convolution fusion | flops 268959744 | bytes 1572876 | tf_op jit(solution)/shard_map/while/body/dot_general | solution.py:42
  113.2 0.0 copy-start.1
  113.3 1.0 copy-done.1
Async XLA Ops:
  6.5 1.0 copy-start
  6.5 33.2 %all-gather.2.cloned.1.call-start = ((), (), s32[]{:S(2)}) async-start(), calls=%async_computation | async-start | bytes 2359296 | tf_op jit(solution)/shard_map/all_gather | solution.py:22
  9.6 85.5 %all-reduce.2.cloned.1.call-start = ((), (), s32[]{:S(2)}) async-start(), calls=%async_computation.1 | async-start | bytes 2097152 | tf_op jit(solution)/shard_map/psum | solution.py:9
  39.8 55.3 %copy-start.2 = (s32[1,1,2]{2,1,0:T(1,128)S(1)}, s32[1,1,2]{2,1,0:T(1,128)}, u32[]{:S(2)}) copy-start(s32[1,1,2]{2,1,0:T(1,128)} %param.9) | copy-start | bytes 28
  39.8 55.3 %copy-start.3 = (s32[1,1,2]{2,1,0:T(1,128)S(1)}, s32[1,1,2]{2,1,0:T(1,128)}, u32[]{:S(2)}) copy-start(s32[1,1,2]{2,1,0:T(1,128)} %param.10) | copy-start | bytes 28
  113.2 1.0 copy-start.1
Sparse Core Ops, SparseCore 0:
  9.7 30.0 all-gather.1
  42.8 52.1 all-reduce.1
where the time goes:
time: 122 us; the launch traced here: 121 us
  waiting for transfers between devices  83.1 us (68%)
  between operations  13.5 us (11%)
  loops' own time  12.4 us (10%)
  matrix products  5.3 us (4%)
  local copies, waits for them, and re-layouts  4.43 us (4%)
  other arithmetic  2.29 us (2%)
    psum x1, waiting for transfers between devices, broadcast(): return lax.psum(kept, axis)  52.9 us
    all_gather x1, waiting for transfers between devices, body(): lax.all_gather(solved, 'col', axis=2, tiled=True)  30.2 us
    another operation x1, loops' own time, body(): result = lax.fori_loop(0, live_here, update, result)  12.4 us
    dot_general x2, matrix products, update(): lax.dot_general(left_tile, right_tile, (((1,), (1,)), ((), ())), preferre...  3.35 us
  transfers between devices with their start and end apart: 2, of which 2 were waited for; matrix products, arithmetic and copies ran while one was open for 0% of the time, Pallas kernels for 0%

commit v1 on v0

v1 whole, which is shorter than its diff:
```python
import functools
import math

import jax
import jax.numpy as jnp
from jax import lax
from jax.experimental import pallas as pl
from jax.experimental.pallas import tpu as pltpu
from jax.sharding import PartitionSpec as P

MESH = pl.DeviceIdType.MESH


def row_sides(grid_rows):
    width = math.isqrt(grid_rows)
    while grid_rows % width:
        width -= 1
    return grid_rows // width, width


def kernel(
    grid_rows,
    grid_cols,
    panel_ref,
    inverse_ref,
    slot_rows_ref,
    slot_cols_ref,
    live_ref,
    out_ref,
    panel_buf,
    inverse_buf,
    rows,
    cols,
    result,
    load_sem,
    store_sem,
    local_sem,
    up_send,
    up_recv,
    down_send,
    down_recv,
    sib_send,
    sib_recv,
    y_send,
    x_send,
    col_recv,
):
    depth = grid_cols // 2
    height, width = row_sides(grid_rows)
    column_count, col_ratio, tile, _ = rows.shape
    part = tile // grid_cols
    slot_total = result.shape[0]

    r = lax.axis_index("row")
    c = lax.axis_index("col")
    y, x = r // width, lax.rem(r, width)
    z, core = c // 2, lax.rem(c, 2)
    other = 1 - core
    own_group = c // grid_rows
    source = lax.rem(c, grid_rows)
    source_y, source_x = source // width, lax.rem(source, width)
    is_source = r == source
    on_source_x = x == source_x
    relays = jnp.logical_and(on_source_x, y != source_y)

    load_panel = pltpu.make_async_copy(panel_ref, panel_buf, load_sem.at[0])
    load_inverse = pltpu.make_async_copy(inverse_ref, inverse_buf, load_sem.at[1])
    load_panel.start()
    load_inverse.start()

    barrier = pltpu.get_barrier_semaphore()

    def greet(row, col):
        pl.semaphore_signal(barrier, inc=1, device_id=(row, col), device_id_type=MESH)

    greet(r, 2 * z + other)
    for step in range(1, width):
        greet(y * width + lax.rem(x + step, width), c)
    for step in range(1, height):
        greet(lax.rem(y + step, height) * width + x, c)
    can_up, can_down = z + 1 < depth, z > 0

    @pl.when(can_up)
    def _():
        greet(r, c + 2)

    @pl.when(can_down)
    def _():
        greet(r, c - 2)

    def band(piece):
        return pl.ds(pl.multiple_of(piece * part, part), part)

    load_panel.wait()
    load_inverse.wait()
    solved = jnp.dot(
        panel_buf[...].reshape(-1, tile), inverse_buf[...], preferred_element_type=jnp.float32
    )
    solved = solved.astype(jnp.bfloat16).reshape(column_count, col_ratio, part, tile)
    rows[:, :, band(c), :] = solved

    line_peers = can_up.astype(jnp.int32) + can_down.astype(jnp.int32)
    pl.semaphore_wait(barrier, 1 + (width - 1) + (height - 1) + line_peers)

    def up(dist, group):
        chunk = rows.at[:, group, band(c - 2 * dist)]
        return pltpu.make_async_remote_copy(
            chunk, chunk, up_send.at[dist, group], up_recv.at[dist, group], (r, c + 2), MESH
        )

    def up_arrival(dist, group):
        chunk = rows.at[:, group, band(c - 2 * dist)]
        return pltpu.make_async_remote_copy(
            chunk, chunk, up_send.at[dist, group], up_recv.at[dist - 1, group], (r, c - 2), MESH
        )

    def down(dist, group):
        chunk = rows.at[:, group, band(c + 2 * dist)]
        return pltpu.make_async_remote_copy(
            chunk, chunk, down_send.at[dist, group], down_recv.at[dist, group], (r, c - 2), MESH
        )

    def down_arrival(dist, group):
        chunk = rows.at[:, group, band(c + 2 * dist)]
        return pltpu.make_async_remote_copy(
            chunk, chunk, down_send.at[dist, group], down_recv.at[dist - 1, group], (r, c + 2), MESH
        )

    def sibling(level, group, sender):
        chunk = rows.at[:, group, band(2 * level + sender)]
        return pltpu.make_async_remote_copy(
            chunk,
            chunk,
            sib_send.at[level, group],
            sib_recv.at[level, group],
            (r, 2 * z + other),
            MESH,
        )

    def along_y(piece, step):
        return pltpu.make_async_remote_copy(
            rows.at[:, own_group, band(piece)],
            cols.at[:, band(piece)],
            y_send.at[step - 1, piece],
            col_recv.at[piece],
            (lax.rem(y + step, height) * width + x, c),
            MESH,
        )

    def along_x(piece, step, origin):
        return pltpu.make_async_remote_copy(
            origin,
            cols.at[:, band(piece)],
            x_send.at[step - 1, piece],
            col_recv.at[piece],
            (y * width + lax.rem(x + step, width), c),
            MESH,
        )

    def keep(piece):
        return pltpu.make_async_copy(
            rows.at[:, own_group, band(piece)], cols.at[:, band(piece)], local_sem.at[piece]
        )

    def column_send(piece):
        for step in range(1, height):
            along_y(piece, step).start()
        for step in range(1, width):
            along_x(piece, step, rows.at[:, own_group, band(piece)]).start()
        keep(piece).start()

    def column_arrival(piece):
        return along_x(piece, 1, cols.at[:, band(piece)])

    def column_relay(piece):
        column_arrival(piece).wait_recv()
        for step in range(1, width):
            along_x(piece, step, cols.at[:, band(piece)]).start()

    def levels(dist):
        if dist == 0:
            return [(z, None)]
        return [(z - dist, z >= dist), (z + dist, z + dist < depth)]

    def guarded(condition, action):
        if condition is None:
            action()
        else:
            pl.when(condition)(action)

    def column_step(dist, sender):
        for level, exists in levels(dist):

            def act(level=level):
                if sender is other:
                    for group in range(col_ratio):
                        sibling(level, group, other).wait_recv()

                @pl.when(is_source)
                def _():
                    column_send(2 * level + sender)

            guarded(exists, act)

    def relay_step(dist):
        for level, exists in levels(dist):

            def act(level=level):
                @pl.when(relays)
                def _():
                    column_relay(2 * level)
                    column_relay(2 * level + 1)

            guarded(exists, act)

    for turn in range(col_ratio):
        high, low = col_ratio - 1 - turn, turn

        @pl.when(can_up)
        def _():
            up(0, high).start()

        @pl.when(can_down)
        def _():
            down(0, low).start()

    for group in range(col_ratio):
        sibling(z, group, core).start()
    column_step(0, core)

    for dist in range(1, depth):
        for turn in range(col_ratio):
            high, low = col_ratio - 1 - turn, turn

            @pl.when(z >= dist)
            def _():
                up_arrival(dist, high).wait_recv()

                @pl.when(can_up)
                def _():
                    up(dist, high).start()

                sibling(z - dist, high, core).start()

            @pl.when(z + dist < depth)
            def _():
                down_arrival(dist, low).wait_recv()

                @pl.when(can_down)
                def _():
                    down(dist, low).start()

                sibling(z + dist, low, core).start()

        column_step(dist, core)
        column_step(dist - 1, other)
        relay_step(dist - 1)
    column_step(depth - 1, other)
    relay_step(depth - 1)

    @pl.when(jnp.logical_not(on_source_x))
    def _():
        for piece in range(grid_cols):
            column_arrival(piece).wait_recv()

    @pl.when(is_source)
    def _():
        for piece in range(grid_cols):
            keep(piece).wait()

    for slot in range(slot_total):
        left = slot_rows_ref[0, 0, slot] // grid_rows
        right = slot_cols_ref[0, 0, slot] // grid_cols
        product = lax.dot_general(
            rows[left // col_ratio, lax.rem(left, col_ratio)],
            cols[right],
            (((1,), (1,)), ((), ())),
            preferred_element_type=jnp.float32,
        )
        live = slot < live_ref[0, 0]
        result[slot] = jnp.where(live, -product, 0.0).astype(result.dtype)
        pltpu.make_async_copy(result.at[slot], out_ref.at[0, 0, slot], store_sem.at[slot]).start()

    for dist in range(depth):
        for group in range(col_ratio):

            @pl.when(jnp.logical_and(can_up, z >= dist))
            def _():
                up(dist, group).wait_send()

            @pl.when(jnp.logical_and(can_down, z + dist < depth))
            def _():
                down(dist, group).wait_send()

    for level in range(depth):
        for group in range(col_ratio):
            sibling(level, group, core).wait_send()

    for piece in range(grid_cols):

        @pl.when(is_source)
        def _():
            for step in range(1, height):
                along_y(piece, step).wait_send()

        @pl.when(on_source_x)
        def _():
            for step in range(1, width):
                along_x(piece, step, cols.at[:, band(piece)]).wait_send()

    for slot in range(slot_total):
        pltpu.make_async_copy(result.at[slot], out_ref.at[0, 0, slot], store_sem.at[slot]).wait()


def body(grid_rows, grid_cols, panel, inverse_factor, slot_rows, slot_cols, live_count):
    panel_count, _, part_rows, tile = panel.shape
    slot_total = slot_rows.shape[-1]
    col_ratio = grid_cols // grid_rows
    column_count = panel_count // col_ratio
    depth = grid_cols // 2
    height, width = row_sides(grid_rows)
    dma = pltpu.SemaphoreType.DMA
    flops = 2 * tile * tile * (panel_count * part_rows + slot_total * tile)
    return pl.pallas_call(
        functools.partial(kernel, grid_rows, grid_cols),
        out_shape=jax.ShapeDtypeStruct((1, 1, slot_total, tile, tile), jnp.bfloat16),
        in_specs=[pl.BlockSpec(memory_space=pl.ANY)] * 2
        + [pl.BlockSpec(memory_space=pltpu.SMEM)] * 3,
        out_specs=pl.BlockSpec(memory_space=pl.ANY),
        scratch_shapes=[
            pltpu.VMEM(panel.shape, jnp.bfloat16),
            pltpu.VMEM(inverse_factor.shape, jnp.bfloat16),
            pltpu.VMEM((column_count, col_ratio, tile, tile), jnp.bfloat16),
            pltpu.VMEM((column_count, tile, tile), jnp.bfloat16),
            pltpu.VMEM((slot_total, tile, tile), jnp.bfloat16),
            dma((2,)),
            dma((slot_total,)),
            dma((grid_cols,)),
            dma((depth, col_ratio)),
            dma((depth, col_ratio)),
            dma((depth, col_ratio)),
            dma((depth, col_ratio)),
            dma((depth, col_ratio)),
            dma((depth, col_ratio)),
            dma((max(height - 1, 1), grid_cols)),
            dma((max(width - 1, 1), grid_cols)),
            dma((grid_cols,)),
        ],
        compiler_params=pltpu.CompilerParams(
            collective_id=0, has_side_effects=True, vmem_limit_bytes=32 * 1024 * 1024
        ),
        cost_estimate=pl.CostEstimate(
            flops=flops, bytes_accessed=2 * tile * tile * (1 + slot_total), transcendentals=0
        ),
    )(panel, inverse_factor, slot_rows, slot_cols, live_count)


def solution(mesh):
    placed = (
        P(None, "row", "col", None),
        P(),
        P("row", "col", None),
        P("row", "col", None),
        P("row", "col"),
    )
    return jax.shard_map(
        functools.partial(body, mesh.shape["row"], mesh.shape["col"]),
        mesh=mesh,
        in_specs=placed,
        out_specs=P("row", "col", None, None, None),
        check_vma=False,
    )
```

time: 122 us -> 41 us (0.34)
  the two profiles are of different devices: /device:TPU:17 before, /device:TPU:5 now
where the time goes in v1:
time: 41 us; the launch traced here: 40.3 us
  Pallas kernels  36.6 us (89%)
  local copies, waits for them, and re-layouts  2.96 us (7%)
  between operations  0.71 us (2%)
    pallas_call x1, Pallas kernels, body(): pl.pallas_call(functools.partial(kernel, grid_rows, grid_cols), out_shape...  36.6 us
    unnamed x9, local copies, waits for them, and re-layouts  2.96 us

profile of v1, /device:TPU:5, one launch (start us, length us, event | category | flops | bytes accessed | tf_op | source)
XLA Modules:
  0.0 40.3 jit_solution(14673418308596115817)
XLA Ops:
  0.0 0.0 copy-start.3
  0.0 0.0 copy-start.2
  0.7 0.0 copy-done.3
  0.7 0.0 copy-done.2
  0.7 0.0 copy-start
  0.7 1.0 %copy-done = bf16[512,512]{1,0:T(8,128)(2,1)S(1)} copy-done((bf16[512,512]{1,0:T(8,128)(2,1)S(1)}, bf16[512,512]{1,0:T(8,128)(2,1)}, u32[]{:S(2)}) %copy-start) | copy-done | bytes 524312
  1.7 0.0 copy-start.1
  1.7 0.9 %copy-done.1 = bf16[4,1,64,512]{3,2,1,0:T(8,128)(2,1)S(1)} copy-done((bf16[4,1,64,512]{3,2,1,0:T(8,128)(2,1)S(1)}, bf16[4,1,64,512]{3,2,1,0:T(8,128)(2,1)}, u32[]{:S(2)}) %copy-start.1) | copy-done | bytes 262168
  2.7 36.6 %shard_map.55 = bf16[1,1,2,512,512]{4,3,2,1,0:T(8,128)(2,1)S(1)} custom-call(bf16[4,1,64,512]{3,2,1,0:T(8,128)(2,1)S(1)} %copy-done.1, bf16[512,512]{1,0:T(8,128)(2,1)S(1)} %copy-done, s32[1,1,2]{2,1,0:T(1,128)S(1)} %copy-done.2, s32[1,1,2]{2,1,0:T(1,128)S(1)} %copy-done.3, s32[1,1]{1,0:T(1,128)S(6)} %copy.7.live_ref), custom_call_target="tpu_custom_call" | custom-call | flops 671088640 | bytes 1572864 | tf_op jit(solution)/shard_map/pallas_call | solution.py:324
  39.3 1.0 %copy.8 = bf16[1,1,2,512,512]{4,3,2,1,0:T(8,128)(2,1)} copy(bf16[1,1,2,512,512]{4,3,2,1,0:T(8,128)(2,1)S(1)} %shard_map.55) | data formatting | bytes 2097152
Async XLA Ops:
  0.0 0.7 %copy-start.3 = (s32[1,1,2]{2,1,0:T(1,128)S(1)}, s32[1,1,2]{2,1,0:T(1,128)}, u32[]{:S(2)}) copy-start(s32[1,1,2]{2,1,0:T(1,128)} %slot_cols_ref.1) | copy-start | bytes 28
  0.0 0.7 %copy-start.2 = (s32[1,1,2]{2,1,0:T(1,128)S(1)}, s32[1,1,2]{2,1,0:T(1,128)}, u32[]{:S(2)}) copy-start(s32[1,1,2]{2,1,0:T(1,128)} %slot_rows_ref.1) | copy-start | bytes 28
  0.7 1.0 %copy-start = (bf16[512,512]{1,0:T(8,128)(2,1)S(1)}, bf16[512,512]{1,0:T(8,128)(2,1)}, u32[]{:S(2)}) copy-start(bf16[512,512]{1,0:T(8,128)(2,1)} %inverse_ref.1) | copy-start | bytes 1572868
  1.7 0.9 %copy-start.1 = (bf16[4,1,64,512]{3,2,1,0:T(8,128)(2,1)S(1)}, bf16[4,1,64,512]{3,2,1,0:T(8,128)(2,1)}, u32[]{:S(2)}) copy-start(bf16[4,1,64,512]{3,2,1,0:T(8,128)(2,1)} %panel_ref.1) | copy-start | bytes 786436

commit v2 on v1

v2 whole, which is shorter than its diff:
```python
import functools
import math

import jax
import jax.numpy as jnp
from jax import lax
from jax.experimental import pallas as pl
from jax.experimental.pallas import tpu as pltpu
from jax.sharding import PartitionSpec as P

MESH = pl.DeviceIdType.MESH


def row_sides(grid_rows):
    width = math.isqrt(grid_rows)
    while grid_rows % width:
        width -= 1
    return grid_rows // width, width


def kernel(
    grid_rows,
    grid_cols,
    panel_ref,
    inverse_ref,
    slot_rows_ref,
    slot_cols_ref,
    live_ref,
    out_ref,
    panel_buf,
    inverse_buf,
    slot_rows,
    slot_cols,
    live,
    rows,
    cols,
    result,
    load_sem,
    store_sem,
    local_sem,
    up_send,
    up_recv,
    down_send,
    down_recv,
    sib_send,
    sib_recv,
    y_send,
    x_send,
    col_recv,
):
    depth = grid_cols // 2
    height, width = row_sides(grid_rows)
    panel_count, tile, _ = rows.shape
    column_count = cols.shape[0]
    col_ratio = panel_count // column_count
    part = tile // grid_cols
    slot_total = result.shape[0]

    r = lax.axis_index("row")
    c = lax.axis_index("col")
    y, x = r // width, lax.rem(r, width)
    z, core = c // 2, lax.rem(c, 2)
    other = 1 - core
    own_group = c // grid_rows
    source = lax.rem(c, grid_rows)
    source_y, source_x = source // width, lax.rem(source, width)
    is_source = r == source
    on_source_x = x == source_x
    relays = jnp.logical_and(on_source_x, y != source_y)

    load_panel = pltpu.make_async_copy(panel_ref, panel_buf, load_sem.at[0])
    load_inverse = pltpu.make_async_copy(inverse_ref, inverse_buf, load_sem.at[1])
    load_panel.start()
    load_inverse.start()
    small = [(slot_rows_ref, slot_rows), (slot_cols_ref, slot_cols), (live_ref, live)]
    small_loads = [
        pltpu.make_async_copy(source_ref, target, load_sem.at[2 + at])
        for at, (source_ref, target) in enumerate(small)
    ]
    for load in small_loads:
        load.start()

    barrier = pltpu.get_barrier_semaphore()

    def greet(row, col):
        pl.semaphore_signal(barrier, inc=1, device_id=(row, col), device_id_type=MESH)

    greet(r, 2 * z + other)
    for step in range(1, width):
        greet(y * width + lax.rem(x + step, width), c)
    for step in range(1, height):
        greet(lax.rem(y + step, height) * width + x, c)
    can_up, can_down = z + 1 < depth, z > 0

    @pl.when(can_up)
    def _():
        greet(r, c + 2)

    @pl.when(can_down)
    def _():
        greet(r, c - 2)

    def band(piece):
        return pl.ds(pl.multiple_of(piece * part, part), part)

    load_panel.wait()
    load_inverse.wait()
    solved = jnp.dot(
        panel_buf[...].reshape(-1, tile), inverse_buf[...], preferred_element_type=jnp.float32
    )
    solved = solved.astype(jnp.bfloat16).reshape(panel_count, part, tile)
    rows[:, band(c), :] = solved

    line_peers = can_up.astype(jnp.int32) + can_down.astype(jnp.int32)
    pl.semaphore_wait(barrier, 1 + (width - 1) + (height - 1) + line_peers)

    def needed(level, a):
        return grid_rows * a + r >= 2 * level

    def guarded(condition, action):
        if condition is None:
            action()
        else:
            pl.when(condition)(action)

    def chunk_of(a, piece):
        return rows.at[a, band(piece)]

    def up(dist, a, ahead=0):
        chunk = chunk_of(a, c - 2 * dist)
        return pltpu.make_async_remote_copy(
            chunk, chunk, up_send.at[dist, a], up_recv.at[dist - ahead, a], (r, c + 2), MESH
        )

    def down(dist, a, ahead=0):
        chunk = chunk_of(a, c + 2 * dist)
        return pltpu.make_async_remote_copy(
            chunk, chunk, down_send.at[dist, a], down_recv.at[dist - ahead, a], (r, c - 2), MESH
        )

    def sibling(level, a, sender):
        chunk = chunk_of(a, 2 * level + sender)
        return pltpu.make_async_remote_copy(
            chunk,
            chunk,
            sib_send.at[level, a],
            sib_recv.at[level, a],
            (r, 2 * z + other),
            MESH,
        )

    def own_tile(k):
        return k * col_ratio + own_group

    def along_y(piece, k, step):
        return pltpu.make_async_remote_copy(
            chunk_of(own_tile(k), piece),
            cols.at[k, band(piece)],
            y_send.at[step - 1, piece, k],
            col_recv.at[piece, k],
            (lax.rem(y + step, height) * width + x, c),
            MESH,
        )

    def along_x(piece, k, step, relayed):
        return pltpu.make_async_remote_copy(
            cols.at[k, band(piece)] if relayed else chunk_of(own_tile(k), piece),
            cols.at[k, band(piece)],
            x_send.at[step - 1, piece, k],
            col_recv.at[piece, k],
            (y * width + lax.rem(x + step, width), c),
            MESH,
        )

    def keep(piece, k):
        return pltpu.make_async_copy(
            chunk_of(own_tile(k), piece), cols.at[k, band(piece)], local_sem.at[piece, k]
        )

    def column_send(piece, k, group):
        @pl.when(jnp.logical_and(is_source, own_group == group))
        def _():
            for step in range(1, height):
                along_y(piece, k, step).start()
            for step in range(1, width):
                along_x(piece, k, step, False).start()
            keep(piece, k).start()

    def column_arrival(piece, k):
        return along_x(piece, k, 1, True)

    def group_of(upward, phase):
        return col_ratio - 1 - phase if upward else phase

    def own_step(phase):
        for k in range(column_count):
            a = k * col_ratio + group_of(True, phase)
            pl.when(jnp.logical_and(can_up, needed(z + 1, a)))(lambda a=a: up(0, a).start())
            a = k * col_ratio + group_of(False, phase)
            pl.when(can_down)(lambda a=a: down(0, a).start())

    def arrive(dist, phase):
        for k in range(column_count):

            def from_below(group=group_of(True, phase), k=k):
                a = k * col_ratio + group
                up(dist, a, 1).wait_recv()
                pl.when(jnp.logical_and(can_up, needed(z + 1, a)))(lambda: up(dist, a).start())
                sibling(z - dist, a, core).start()
                column_send(c - 2 * dist, k, group)

            def from_above(group=group_of(False, phase), k=k):
                a = k * col_ratio + group
                down(dist, a, 1).wait_recv()
                pl.when(can_down)(lambda: down(dist, a).start())
                pl.when(needed(z, a))(lambda: sibling(z + dist, a, core).start())
                column_send(c + 2 * dist, k, group)

            a = k * col_ratio + group_of(True, phase)
            pl.when(jnp.logical_and(z >= dist, needed(z, a)))(from_below)
            pl.when(z + dist < depth)(from_above)

    def sibling_step(dist, phase):
        sides = [(True, z - dist, z >= dist), (False, z + dist, z + dist < depth)]
        for upward, level, exists in sides[: 1 if dist == 0 else 2]:
            for k in range(column_count):

                def act(group=group_of(upward, phase), level=level, k=k):
                    a = k * col_ratio + group

                    @pl.when(needed(z, a))
                    def _():
                        sibling(level, a, other).wait_recv()
                        column_send(2 * level + other, k, group)

                guarded(exists if dist else None, act)

    def relay_step(dist):
        sides = [(z - dist, z >= dist), (z + dist, z + dist < depth)]
        for level, exists in sides[: 1 if dist == 0 else 2]:

            def act(level=level):
                @pl.when(relays)
                def _():
                    for sender in range(2):
                        piece = 2 * level + sender
                        for k in range(column_count):
                            column_arrival(piece, k).wait_recv()
                            for step in range(1, width):
                                along_x(piece, k, step, True).start()

            guarded(exists if dist else None, act)

    phases = range(1, col_ratio)
    own_step(0)
    for a in range(panel_count):
        pl.when(needed(z, a))(lambda a=a: sibling(z, a, core).start())
    for k in range(column_count):
        for group in range(col_ratio):
            column_send(c, k, group)

    for dist in range(1, depth):
        arrive(dist, 0)
        for phase in phases:
            if dist == 1:
                own_step(phase)
            else:
                arrive(dist - 1, phase)
        sibling_step(dist - 1, 0)
        if dist == 1:
            for phase in phases:
                sibling_step(0, phase)
        else:
            for phase in phases if dist > 2 else ():
                sibling_step(dist - 2, phase)
            relay_step(dist - 2)
    sibling_step(depth - 1, 0)
    for phase in phases:
        sibling_step(depth - 2, phase)
    relay_step(depth - 2)
    relay_step(depth - 1)
    for phase in phases:
        arrive(depth - 1, phase)
    for phase in phases:
        sibling_step(depth - 1, phase)

    @pl.when(jnp.logical_not(on_source_x))
    def _():
        for piece in range(grid_cols):
            for k in range(column_count):
                column_arrival(piece, k).wait_recv()

    @pl.when(is_source)
    def _():
        for piece in range(grid_cols):
            for k in range(column_count):
                keep(piece, k).wait()

    for load in small_loads:
        load.wait()
    for slot in range(slot_total):
        left = slot_rows[0, 0, slot] // grid_rows
        right = slot_cols[0, 0, slot] // grid_cols
        product = lax.dot_general(
            rows[left],
            cols[right],
            (((1,), (1,)), ((), ())),
            preferred_element_type=jnp.float32,
        )
        alive = slot < live[0, 0]
        result[slot] = jnp.where(alive, -product, 0.0).astype(result.dtype)
        pltpu.make_async_copy(result.at[slot], out_ref.at[0, 0, slot], store_sem.at[slot]).start()

    for a in range(panel_count):
        for dist in range(depth):
            sent_up = jnp.logical_and(jnp.logical_and(can_up, z >= dist), needed(z + 1, a))
            pl.when(sent_up)(lambda a=a, dist=dist: up(dist, a).wait_send())
            sent_down = jnp.logical_and(can_down, z + dist < depth)
            pl.when(sent_down)(lambda a=a, dist=dist: down(dist, a).wait_send())

        @pl.when(needed(z, a))
        def _(a=a):
            for level in range(depth):
                sibling(level, a, core).wait_send()

    @pl.when(is_source)
    def _():
        for piece in range(grid_cols):
            for k in range(column_count):
                for step in range(1, height):
                    along_y(piece, k, step).wait_send()

    @pl.when(on_source_x)
    def _():
        for piece in range(grid_cols):
            for k in range(column_count):
                for step in range(1, width):
                    along_x(piece, k, step, True).wait_send()

    for slot in range(slot_total):
        pltpu.make_async_copy(result.at[slot], out_ref.at[0, 0, slot], store_sem.at[slot]).wait()


def body(grid_rows, grid_cols, panel, inverse_factor, slot_rows, slot_cols, live_count):
    panel_count, _, part_rows, tile = panel.shape
    slot_total = slot_rows.shape[-1]
    col_ratio = grid_cols // grid_rows
    column_count = panel_count // col_ratio
    depth = grid_cols // 2
    height, width = row_sides(grid_rows)
    dma = pltpu.SemaphoreType.DMA
    flops = 2 * tile * tile * (panel_count * part_rows + slot_total * tile)
    return pl.pallas_call(
        functools.partial(kernel, grid_rows, grid_cols),
        out_shape=jax.ShapeDtypeStruct((1, 1, slot_total, tile, tile), jnp.bfloat16),
        in_specs=[pl.BlockSpec(memory_space=pl.ANY)] * 5,
        out_specs=pl.BlockSpec(memory_space=pl.ANY),
        scratch_shapes=[
            pltpu.VMEM(panel.shape, jnp.bfloat16),
            pltpu.VMEM(inverse_factor.shape, jnp.bfloat16),
            pltpu.SMEM(slot_rows.shape, jnp.int32),
            pltpu.SMEM(slot_cols.shape, jnp.int32),
            pltpu.SMEM(live_count.shape, jnp.int32),
            pltpu.VMEM((panel_count, tile, tile), jnp.bfloat16),
            pltpu.VMEM((column_count, tile, tile), jnp.bfloat16),
            pltpu.VMEM((slot_total, tile, tile), jnp.bfloat16),
            dma((5,)),
            dma((slot_total,)),
            dma((grid_cols, column_count)),
            dma((depth, panel_count)),
            dma((depth, panel_count)),
            dma((depth, panel_count)),
            dma((depth, panel_count)),
            dma((depth, panel_count)),
            dma((depth, panel_count)),
            dma((max(height - 1, 1), grid_cols, column_count)),
            dma((max(width - 1, 1), grid_cols, column_count)),
            dma((grid_cols, column_count)),
        ],
        compiler_params=pltpu.CompilerParams(
            collective_id=0, has_side_effects=True, vmem_limit_bytes=32 * 1024 * 1024
        ),
        cost_estimate=pl.CostEstimate(
            flops=flops, bytes_accessed=2 * tile * tile * (1 + slot_total), transcendentals=0
        ),
    )(panel, inverse_factor, slot_rows, slot_cols, live_count)


def solution(mesh):
    placed = (
        P(None, "row", "col", None),
        P(),
        P("row", "col", None),
        P("row", "col", None),
        P("row", "col"),
    )
    return jax.shard_map(
        functools.partial(body, mesh.shape["row"], mesh.shape["col"]),
        mesh=mesh,
        in_specs=placed,
        out_specs=P("row", "col", None, None, None),
        check_vma=False,
    )
```

time: 41 us -> 36.9 us (0.90)
  the two profiles are of different devices: /device:TPU:5 before, /device:TPU:6 now
where the time goes in v2:
time: 36.9 us; the launch traced here: 36.7 us
  Pallas kernels  33 us (89%)
  local copies, waits for them, and re-layouts  2.96 us (8%)
  between operations  0.71 us (2%)
    pallas_call x1, Pallas kernels, body(): pl.pallas_call(functools.partial(kernel, grid_rows, grid_cols), out_shape...  33 us
    unnamed x9, local copies, waits for them, and re-layouts  2.96 us

profile of v2, /device:TPU:6, one launch (start us, length us, event | category | flops | bytes accessed | tf_op | source)
XLA Modules:
  0.0 36.7 jit_solution(15646311418721619078)
XLA Ops:
  0.0 0.0 copy-start.3
  0.0 0.0 copy-start.2
  0.7 0.0 copy-done.3
  0.7 0.0 copy-done.2
  0.7 0.0 copy-start
  0.7 1.0 %copy-done = bf16[512,512]{1,0:T(8,128)(2,1)S(1)} copy-done((bf16[512,512]{1,0:T(8,128)(2,1)S(1)}, bf16[512,512]{1,0:T(8,128)(2,1)}, u32[]{:S(2)}) %copy-start) | copy-done | bytes 524312
  1.7 0.0 copy-start.1
  1.7 0.9 %copy-done.1 = bf16[4,1,64,512]{3,2,1,0:T(8,128)(2,1)S(1)} copy-done((bf16[4,1,64,512]{3,2,1,0:T(8,128)(2,1)S(1)}, bf16[4,1,64,512]{3,2,1,0:T(8,128)(2,1)}, u32[]{:S(2)}) %copy-start.1) | copy-done | bytes 262168
  2.7 33.0 %shard_map.55 = bf16[1,1,2,512,512]{4,3,2,1,0:T(8,128)(2,1)S(1)} custom-call(bf16[4,1,64,512]{3,2,1,0:T(8,128)(2,1)S(1)} %copy-done.1, bf16[512,512]{1,0:T(8,128)(2,1)S(1)} %copy-done, s32[1,1,2]{2,1,0:T(1,128)S(1)} %copy-done.2, s32[1,1,2]{2,1,0:T(1,128)S(1)} %copy-done.3, s32[1,1]{1,0:T(1,128)S(6)} %copy.7.live_ref), custom_call_target="tpu_custom_call" | custom-call | flops 671088640 | bytes 1572864 | tf_op jit(solution)/shard_map/pallas_call | solution.py:353
  35.7 1.0 %copy.8 = bf16[1,1,2,512,512]{4,3,2,1,0:T(8,128)(2,1)} copy(bf16[1,1,2,512,512]{4,3,2,1,0:T(8,128)(2,1)S(1)} %shard_map.55) | data formatting | bytes 2097152
Async XLA Ops:
  0.0 0.7 %copy-start.3 = (s32[1,1,2]{2,1,0:T(1,128)S(1)}, s32[1,1,2]{2,1,0:T(1,128)}, u32[]{:S(2)}) copy-start(s32[1,1,2]{2,1,0:T(1,128)} %slot_cols_ref.1) | copy-start | bytes 28
  0.0 0.7 %copy-start.2 = (s32[1,1,2]{2,1,0:T(1,128)S(1)}, s32[1,1,2]{2,1,0:T(1,128)}, u32[]{:S(2)}) copy-start(s32[1,1,2]{2,1,0:T(1,128)} %slot_rows_ref.1) | copy-start | bytes 28
  0.7 1.0 %copy-start = (bf16[512,512]{1,0:T(8,128)(2,1)S(1)}, bf16[512,512]{1,0:T(8,128)(2,1)}, u32[]{:S(2)}) copy-start(bf16[512,512]{1,0:T(8,128)(2,1)} %inverse_ref.1) | copy-start | bytes 1572868
  1.7 0.9 %copy-start.1 = (bf16[4,1,64,512]{3,2,1,0:T(8,128)(2,1)S(1)}, bf16[4,1,64,512]{3,2,1,0:T(8,128)(2,1)}, u32[]{:S(2)}) copy-start(bf16[4,1,64,512]{3,2,1,0:T(8,128)(2,1)} %panel_ref.1) | copy-start | bytes 786436

commit v3 on v2

--- a/solution.py
+++ b/solution.py
@@ -266,18 +266,10 @@
                 own_step(phase)
             else:
                 arrive(dist - 1, phase)
-        sibling_step(dist - 1, 0)
-        if dist == 1:
-            for phase in phases:
-                sibling_step(0, phase)
-        else:
-            for phase in phases if dist > 2 else ():
-                sibling_step(dist - 2, phase)
-            relay_step(dist - 2)
+        for phase in range(col_ratio):
+            sibling_step(dist - 1, phase)
+        relay_step(dist - 1)
     sibling_step(depth - 1, 0)
-    for phase in phases:
-        sibling_step(depth - 2, phase)
-    relay_step(depth - 2)
     relay_step(depth - 1)
     for phase in phases:
         arrive(depth - 1, phase)
@@ -353,7 +345,7 @@
     return pl.pallas_call(
         functools.partial(kernel, grid_rows, grid_cols),
         out_shape=jax.ShapeDtypeStruct((1, 1, slot_total, tile, tile), jnp.bfloat16),
-        in_specs=[pl.BlockSpec(memory_space=pl.ANY)] * 5,
+        in_specs=[pl.BlockSpec(memory_space=pltpu.HBM)] * 5,
         out_specs=pl.BlockSpec(memory_space=pl.ANY),
         scratch_shapes=[
             pltpu.VMEM(panel.shape, jnp.bfloat16),

time: 36.9 us -> 35 us (0.949)
  the two profiles are of different devices: /device:TPU:6 before, /device:TPU:5 now
where the time goes in v3:
time: 35 us; the launch traced here: 34.8 us
  Pallas kernels  31.2 us (89%)
  local copies, waits for them, and re-layouts  2.96 us (8%)
  between operations  0.71 us (2%)
    pallas_call x1, Pallas kernels, body(): pl.pallas_call(functools.partial(kernel, grid_rows, grid_cols), out_shape...  31.2 us
    unnamed x9, local copies, waits for them, and re-layouts  2.96 us

profile of v3, /device:TPU:5, one launch (start us, length us, event | category | flops | bytes accessed | tf_op | source)
XLA Modules:
  0.0 34.8 jit_solution(16979604970418620212)
XLA Ops:
  0.0 0.0 copy-start.3
  0.0 0.0 copy-start.2
  0.7 0.0 copy-done.3
  0.7 0.0 copy-done.2
  0.7 0.0 copy-start
  0.7 1.0 %copy-done = bf16[512,512]{1,0:T(8,128)(2,1)S(1)} copy-done((bf16[512,512]{1,0:T(8,128)(2,1)S(1)}, bf16[512,512]{1,0:T(8,128)(2,1)}, u32[]{:S(2)}) %copy-start) | copy-done | bytes 524312
  1.7 0.0 copy-start.1
  1.7 0.9 %copy-done.1 = bf16[4,1,64,512]{3,2,1,0:T(8,128)(2,1)S(1)} copy-done((bf16[4,1,64,512]{3,2,1,0:T(8,128)(2,1)S(1)}, bf16[4,1,64,512]{3,2,1,0:T(8,128)(2,1)}, u32[]{:S(2)}) %copy-start.1) | copy-done | bytes 262168
  2.7 31.2 %shard_map.55 = bf16[1,1,2,512,512]{4,3,2,1,0:T(8,128)(2,1)S(1)} custom-call(bf16[4,1,64,512]{3,2,1,0:T(8,128)(2,1)S(1)} %copy-done.1, bf16[512,512]{1,0:T(8,128)(2,1)S(1)} %copy-done, s32[1,1,2]{2,1,0:T(1,128)S(1)} %copy-done.2, s32[1,1,2]{2,1,0:T(1,128)S(1)} %copy-done.3, s32[1,1]{1,0:T(1,128)S(6)} %copy.7.live_ref), custom_call_target="tpu_custom_call" | custom-call | flops 671088640 | bytes 1572864 | tf_op jit(solution)/shard_map/pallas_call | solution.py:345
  33.9 1.0 %copy.8 = bf16[1,1,2,512,512]{4,3,2,1,0:T(8,128)(2,1)} copy(bf16[1,1,2,512,512]{4,3,2,1,0:T(8,128)(2,1)S(1)} %shard_map.55) | data formatting | bytes 2097152
Async XLA Ops:
  0.0 0.7 %copy-start.3 = (s32[1,1,2]{2,1,0:T(1,128)S(1)}, s32[1,1,2]{2,1,0:T(1,128)}, u32[]{:S(2)}) copy-start(s32[1,1,2]{2,1,0:T(1,128)} %slot_cols_ref.1) | copy-start | bytes 28
  0.0 0.7 %copy-start.2 = (s32[1,1,2]{2,1,0:T(1,128)S(1)}, s32[1,1,2]{2,1,0:T(1,128)}, u32[]{:S(2)}) copy-start(s32[1,1,2]{2,1,0:T(1,128)} %slot_rows_ref.1) | copy-start | bytes 28
  0.7 1.0 %copy-start = (bf16[512,512]{1,0:T(8,128)(2,1)S(1)}, bf16[512,512]{1,0:T(8,128)(2,1)}, u32[]{:S(2)}) copy-start(bf16[512,512]{1,0:T(8,128)(2,1)} %inverse_ref.1) | copy-start | bytes 1572868
  1.7 0.9 %copy-start.1 = (bf16[4,1,64,512]{3,2,1,0:T(8,128)(2,1)S(1)}, bf16[4,1,64,512]{3,2,1,0:T(8,128)(2,1)}, u32[]{:S(2)}) copy-start(bf16[4,1,64,512]{3,2,1,0:T(8,128)(2,1)} %panel_ref.1) | copy-start | bytes 786436

commit v4 on v3

--- a/solution.py
+++ b/solution.py
@@ -235,21 +235,22 @@
 
                 guarded(exists if dist else None, act)
 
-    def relay_step(dist):
-        sides = [(z - dist, z >= dist), (z + dist, z + dist < depth)]
-        for level, exists in sides[: 1 if dist == 0 else 2]:
-
-            def act(level=level):
-                @pl.when(relays)
-                def _():
-                    for sender in range(2):
-                        piece = 2 * level + sender
-                        for k in range(column_count):
-                            column_arrival(piece, k).wait_recv()
-                            for step in range(1, width):
-                                along_x(piece, k, step, True).start()
-
-            guarded(exists if dist else None, act)
+    def relay_step(dist, phase):
+        sides = [(True, z - dist, z >= dist), (False, z + dist, z + dist < depth)]
+        for upward, level, exists in sides[: 1 if dist == 0 else 2]:
+            mine = relays
+            if dist:
+                mine = jnp.logical_and(relays, own_group == group_of(upward, phase))
+                mine = jnp.logical_and(mine, exists)
+
+            @pl.when(mine)
+            def _(level=level):
+                for sender in range(2):
+                    piece = 2 * level + sender
+                    for k in range(column_count):
+                        column_arrival(piece, k).wait_recv()
+                        for step in range(1, width):
+                            along_x(piece, k, step, True).start()
 
     phases = range(1, col_ratio)
     own_step(0)
@@ -261,20 +262,30 @@
 
     for dist in range(1, depth):
         arrive(dist, 0)
+        if dist == 1:
+            for phase in phases:
+                own_step(phase)
+            for phase in range(col_ratio):
+                sibling_step(0, phase)
+        sibling_step(dist, 0)
+        if dist == 1:
+            relay_step(0, 0)
+            continue
+        if dist == 2:
+            relay_step(1, 0)
         for phase in phases:
-            if dist == 1:
-                own_step(phase)
-            else:
-                arrive(dist - 1, phase)
-        for phase in range(col_ratio):
+            arrive(dist - 1, phase)
+        for phase in phases:
             sibling_step(dist - 1, phase)
-        relay_step(dist - 1)
-    sibling_step(depth - 1, 0)
-    relay_step(depth - 1)
+        relay_step(dist, 0)
+        for phase in phases:
+            relay_step(dist - 1, phase)
     for phase in phases:
         arrive(depth - 1, phase)
     for phase in phases:
         sibling_step(depth - 1, phase)
+    for phase in phases:
+        relay_step(depth - 1, phase)
 
     @pl.when(jnp.logical_not(on_source_x))
     def _():
@@ -345,7 +356,7 @@
     return pl.pallas_call(
         functools.partial(kernel, grid_rows, grid_cols),
         out_shape=jax.ShapeDtypeStruct((1, 1, slot_total, tile, tile), jnp.bfloat16),
-        in_specs=[pl.BlockSpec(memory_space=pltpu.HBM)] * 5,
+        in_specs=[pl.BlockSpec(memory_space=pl.ANY)] * 5,
         out_specs=pl.BlockSpec(memory_space=pl.ANY),
         scratch_shapes=[
             pltpu.VMEM(panel.shape, jnp.bfloat16),
@@ -370,7 +381,7 @@
             dma((grid_cols, column_count)),
         ],
         compiler_params=pltpu.CompilerParams(
-            collective_id=0, has_side_effects=True, vmem_limit_bytes=32 * 1024 * 1024
+            collective_id=0, has_side_effects=True, vmem_limit_bytes=60 * 1024 * 1024
         ),
         cost_estimate=pl.CostEstimate(
             flops=flops, bytes_accessed=2 * tile * tile * (1 + slot_total), transcendentals=0

time: 35 us -> 32.6 us (0.931)
  the two profiles are of different devices: /device:TPU:5 before, /device:TPU:1 now
where the time goes in v4:
time: 32.6 us; the launch traced here: 32.4 us
  Pallas kernels  29.5 us (90%)
  local copies, waits for them, and re-layouts  2.26 us (7%)
  between operations  0.66 us (2%)
    pallas_call x1, Pallas kernels, body(): pl.pallas_call(functools.partial(kernel, grid_rows, grid_cols), out_shape...  29.5 us
    unnamed x1, local copies, waits for them, and re-layouts  2.26 us

profile of v4, /device:TPU:1, one launch (start us, length us, event | category | flops | bytes accessed | tf_op | source)
XLA Modules:
  0.0 32.4 jit_solution(15668692889973472948)
XLA Ops:
  0.7 29.5 %shard_map.55 = bf16[1,1,2,512,512]{4,3,2,1,0:T(8,128)(2,1)} custom-call(bf16[4,1,64,512]{3,2,1,0:T(8,128)(2,1)} %panel_ref.1, bf16[512,512]{1,0:T(8,128)(2,1)} %inverse_ref.1, s32[1,1,2]{2,1,0:T(1,128)} %slot_rows_ref.1, s32[1,1,2]{2,1,0:T(1,128)} %slot_cols_ref.1, s32[1,1]{1,0:T(1,128)S(6)} %copy.7.live_ref), custom_call_target="tpu_custom_call" | custom-call | flops 671088640 | bytes 1572864 | tf_op jit(solution)/shard_map/pallas_call | solution.py:356
  30.1 2.3 %copy.8 = bf16[1,1,2,512,512]{4,3,2,1,0:T(8,128)(2,1)} copy(bf16[1,1,2,512,512]{4,3,2,1,0:T(8,128)(2,1)} %shard_map.55) | data formatting | bytes 2097152

commit v5 on v4

--- a/solution.py
+++ b/solution.py
@@ -235,12 +235,12 @@
 
                 guarded(exists if dist else None, act)
 
-    def relay_step(dist, phase):
+    def relay_step(dist, phase, place):
         sides = [(True, z - dist, z >= dist), (False, z + dist, z + dist < depth)]
         for upward, level, exists in sides[: 1 if dist == 0 else 2]:
-            mine = relays
+            mine = jnp.logical_and(relays, place)
             if dist:
-                mine = jnp.logical_and(relays, own_group == group_of(upward, phase))
+                mine = jnp.logical_and(mine, own_group == group_of(upward, phase))
                 mine = jnp.logical_and(mine, exists)
 
             @pl.when(mine)
@@ -253,6 +253,8 @@
                             along_x(piece, k, step, True).start()
 
     phases = range(1, col_ratio)
+    between = jnp.logical_and(can_up, can_down)
+    at_end = jnp.logical_not(between)
     own_step(0)
     for a in range(panel_count):
         pl.when(needed(z, a))(lambda a=a: sibling(z, a, core).start())
@@ -269,23 +271,29 @@
                 sibling_step(0, phase)
         sibling_step(dist, 0)
         if dist == 1:
-            relay_step(0, 0)
+            relay_step(0, 0, z >= 0)
             continue
         if dist == 2:
-            relay_step(1, 0)
+            relay_step(1, 0, at_end)
         for phase in phases:
             arrive(dist - 1, phase)
         for phase in phases:
             sibling_step(dist - 1, phase)
-        relay_step(dist, 0)
+        relay_step(dist - 1, 0, between)
+        if dist > 2:
+            for phase in phases:
+                relay_step(dist - 2, phase, between)
+        relay_step(dist, 0, at_end)
         for phase in phases:
-            relay_step(dist - 1, phase)
+            relay_step(dist - 1, phase, at_end)
     for phase in phases:
         arrive(depth - 1, phase)
     for phase in phases:
         sibling_step(depth - 1, phase)
+    relay_step(depth - 1, 0, between)
     for phase in phases:
-        relay_step(depth - 1, phase)
+        relay_step(depth - 2, phase, between)
+        relay_step(depth - 1, phase, z >= 0)
 
     @pl.when(jnp.logical_not(on_source_x))
     def _():

time: 32.6 us -> 31.4 us (0.963)
  the two profiles are of different devices: /device:TPU:1 before, /device:TPU:5 now
where the time goes in v5:
time: 31.4 us; the launch traced here: 30.9 us
  Pallas kernels  28 us (89%)
  local copies, waits for them, and re-layouts  2.26 us (7%)
  between operations  0.66 us (2%)
    pallas_call x1, Pallas kernels, body(): pl.pallas_call(functools.partial(kernel, grid_rows, grid_cols), out_shape...  28 us
    unnamed x1, local copies, waits for them, and re-layouts  2.26 us

profile of v5, /device:TPU:5, one launch (start us, length us, event | category | flops | bytes accessed | tf_op | source)
XLA Modules:
  0.0 30.9 jit_solution(10075649280911304563)
XLA Ops:
  0.7 28.0 %shard_map.55 = bf16[1,1,2,512,512]{4,3,2,1,0:T(8,128)(2,1)} custom-call(bf16[4,1,64,512]{3,2,1,0:T(8,128)(2,1)} %panel_ref.1, bf16[512,512]{1,0:T(8,128)(2,1)} %inverse_ref.1, s32[1,1,2]{2,1,0:T(1,128)} %slot_rows_ref.1, s32[1,1,2]{2,1,0:T(1,128)} %slot_cols_ref.1, s32[1,1]{1,0:T(1,128)S(6)} %copy.7.live_ref), custom_call_target="tpu_custom_call" | custom-call | flops 671088640 | bytes 1572864 | tf_op jit(solution)/shard_map/pallas_call | solution.py:364
  28.6 2.3 %copy.8 = bf16[1,1,2,512,512]{4,3,2,1,0:T(8,128)(2,1)} copy(bf16[1,1,2,512,512]{4,3,2,1,0:T(8,128)(2,1)} %shard_map.55) | data formatting | bytes 2097152
